TPU v7x, 512 devices: a whole 4x8x8 slice. The times are simulated.
512 devices in a mesh: ctx: 128 (over y, z, core), head: 4 (over x).
Axes of the slice: x: 4, y: 8, z: 8, core: 2. Of those that a mesh axis runs over, the one named last changes fastest.
Arguments:
- queries: bfloat16 [2, 16384, 8192], P(None, ('ctx', 'head')), may hold values from -25 to 25
- keys: bfloat16 [2, 16384, 1024], P(None, ('ctx', 'head')), may hold values from -5.5 to 5.5
- values: bfloat16 [2, 16384, 1024], P(None, ('ctx', 'head')), may hold values from -6 to 6
- doc_lengths: int32 [47], replicated, may hold values from 1 to 1408, 32768 in all
Outputs:
- attended: bfloat16 [2, 16384, 8192], P(None, ('ctx', 'head'))
All inputs are finite; a program needn't handle non-finite values.
Results may differ from a plain program's by a relative error of at most 0.0045.
Values may be sent and summed in bfloat16 or wider, within the bound.
A program may use at most 64 MiB of HBM per device.

v0:
```python
import math

import jax
import jax.numpy as jnp
from jax import lax
from jax.sharding import PartitionSpec as P

HD = 128
REACH = 11


NEG_FILL = -1e30


def partner(block, axis, distance):
    count = lax.axis_size(axis)
    route = []
    for low in range(count):
        high = low | 1 << distance
        if high != low and high < count:
            route += [(low, high), (high, low)]
    return lax.ppermute(block, axis, route)


def shifted(block, axis, distance):
    devices = range(lax.axis_size(axis))
    route = [(i - distance, i) for i in devices if i - distance in devices]
    return lax.ppermute(block, axis, route)


def doc_of(positions, ends):
    return jnp.sum((positions[:, None] >= ends[None, :]).astype(jnp.int32), axis=1)


def attend(query, query_pos, keys, values, key_pos, ends, head_dim):
    rows = query.shape[0]
    kv_count = keys.shape[1] // head_dim
    group = query.shape[1] // head_dim // kv_count
    stride = min(group, 4)
    scale = 1.0 / math.sqrt(head_dim)
    allowed = (
        (doc_of(query_pos, ends)[:, None] == doc_of(key_pos, ends)[None, :])
        & (key_pos[None, :] <= query_pos[:, None])
        & (key_pos[None, :] >= 0)
    )
    pieces = []
    for kv_head in range(kv_count):
        key_head = keys[:, kv_head * head_dim : (kv_head + 1) * head_dim]
        value_head = values[:, kv_head * head_dim : (kv_head + 1) * head_dim]
        for portion in range(group // stride):
            first = (kv_head * group + portion * stride) * head_dim
            query_part = query[:, first : first + stride * head_dim].reshape(rows, stride, head_dim)
            scores = (
                jnp.einsum("rhd,sd->hrs", query_part, key_head, preferred_element_type=jnp.float32)
                * scale
            )
            masked = jnp.where(allowed[None], scores, NEG_FILL)
            top = jnp.max(masked, axis=2, keepdims=True)
            weights = jnp.where(allowed[None], jnp.exp(masked - top), 0.0)
            total = jnp.sum(weights, axis=2)
            mixed = jnp.einsum(
                "hrs,sd->rhd",
                weights.astype(jnp.bfloat16),
                value_head,
                preferred_element_type=jnp.float32,
            )
            pieces.append((mixed / total.T[:, :, None]).reshape(rows, stride * head_dim))
    return jnp.concatenate(pieces, axis=1).astype(jnp.bfloat16)


def half_attention(query, query_start, blocks, ends, head_dim):
    rows = query.shape[0]
    count = blocks.shape[0]
    width = blocks.shape[2] // 2
    query_pos = query_start + jnp.arange(rows, dtype=jnp.int32)
    window = blocks.reshape(count * rows, 2 * width)
    key_pos = query_start - (count - 1) * rows + jnp.arange(count * rows, dtype=jnp.int32)
    return attend(query, query_pos, window[:, :width], window[:, width:], key_pos, ends, head_dim)


def per_device(queries, keys, values, doc_lengths):
    head_dim = HD
    ctx_count = lax.axis_size("ctx")
    ctx_pos = lax.axis_index("ctx")
    reach = min(REACH, ctx_count // 2)
    query_local, key_local, value_local = (
        lax.all_to_all(queries, "head", split_axis=2, concat_axis=1, tiled=True),
        lax.all_to_all(keys, "head", split_axis=2, concat_axis=1, tiled=True),
        lax.all_to_all(values, "head", split_axis=2, concat_axis=1, tiled=True),
    )
    keyval = jnp.concatenate([key_local, value_local], axis=2)
    ends = jnp.cumsum(doc_lengths)
    rows = query_local.shape[1]
    query_width = query_local.shape[2]
    moving = jnp.concatenate([query_local[1], keyval[1]], axis=1)
    for digit in range(ctx_count.bit_length() - 1):
        moving = partner(moving, "ctx", digit)
    query_upper = moving[:, :query_width]
    keyval_upper = moving[:, query_width:]
    keyval_lower = keyval[0]
    held_pair = jnp.stack([keyval_lower, keyval_upper])
    earlier = []
    later = []
    for distance in range(1, reach + 1):
        earlier.append(shifted(keyval_lower, "ctx", distance))
        later.append(shifted(held_pair, "ctx", -distance))
    lower_blocks = jnp.stack(
        [earlier[distance - 1] for distance in range(reach, 0, -1)] + [keyval_lower]
    )
    lower_source = jnp.stack(
        [earlier[-offset - 1] for offset in range(-reach, 0)]
        + [keyval_lower]
        + [later[offset - 1][0] for offset in range(1, reach + 1)]
    )
    upper_source = jnp.stack(
        [keyval_upper] + [later[offset - 1][1] for offset in range(1, reach + 1)]
    )
    back_steps = jnp.arange(reach, -1, -1, dtype=jnp.int32)
    upper_index = 2 * ctx_count - 1 - ctx_pos
    target = upper_index - back_steps
    from_upper = target >= ctx_count
    offsets = jnp.clip(target - ctx_pos + reach, 0, 2 * reach)
    upper_blocks = jnp.where(
        from_upper[:, None, None],
        jnp.take(upper_source, back_steps, axis=0),
        jnp.take(lower_source, offsets, axis=0),
    )
    lower_out = half_attention(query_local[0], ctx_pos * rows, lower_blocks, ends, head_dim)
    upper_out = half_attention(query_upper, upper_index * rows, upper_blocks, ends, head_dim)
    for digit in range(ctx_count.bit_length() - 1):
        upper_out = partner(upper_out, "ctx", digit)
    result = jnp.stack([lower_out, upper_out])
    return lax.all_to_all(result, "head", split_axis=1, concat_axis=2, tiled=True)


def solution(mesh):
    placed = (
        P(None, ("ctx", "head"), None),
        P(None, ("ctx", "head"), None),
        P(None, ("ctx", "head"), None),
        P(),
    )
    return jax.shard_map(
        per_device,
        mesh=mesh,
        in_specs=placed,
        out_specs=P(None, ("ctx", "head"), None),
        check_vma=False,
    )
```

profile of v0, /device:TPU:1, one launch (start us, length us, event | category | flops | bytes accessed | tf_op | source)
XLA Modules:
  0.0 675.2 jit_solution(1722678336049449839)
XLA Ops:
  2.5 4.8 all-to-all-start
  9.7 2.5 all-to-all-done
  12.1 3.3 all-to-all-start.1
  15.5 6.8 %copy.273 = bf16[2,32,8192]{1,0,2:T(2,128)(2,1)} copy(bf16[2,32,8192]{2,1,0:T(8,128)(2,1)S(1)} %copy-done.2) | data formatting | bytes 2097152 | tf_op args[0]
  22.3 6.4 reshape.438
  28.7 4.2 all-to-all-start.2
  34.6 8.0 %all-to-all-done.2 = bf16[4,2,65536]{2,1,0:T(2,128)(2,1)S(1)} async-done(((bf16[4,2,65536]{2,1,0:T(2,128)(2,1)}), bf16[4,2,65536]{2,1,0:T(2,128)(2,1)S(1)}, u32[]{:S(2)}, u32[]{:S(2)}) %all-to-all-start.2) | async-done | bytes 1048608 | tf_op jit(solution)/shard_map/all_to_all | solution.py:87
  42.6 3.5 reshape.439
  46.1 9.8 %copy.347 = bf16[2,32,4,2048]{3,2,1,0:T(4,128)(2,1)S(1)} copy(bf16[2,32,4,2048]{1,0,3,2:T(2,128)(2,1)} %bitcast.374) | data formatting | bytes 2097152 | tf_op jit(solution)/shard_map/all_to_all | solution.py:87
  57.7 10.1 %collective-permute-start.11 = (bf16[128,2560]{1,0:T(8,128)(2,1)S(1)}, bf16[128,2560]{1,0:T(8,128)(2,1)S(1)}, u32[]{:S(2)}, u32[]{:S(2)}) collective-permute-start(bf16[128,2560]{1,0:T(8,128)(2,1)S(1)} %pad_maximum_fusion.1), channel_id=1, source_target_pairs={{0,4},{4,0},{8,12},{12,8},{16,20},{20,16},{24,28},{28,24},{32,36},... | collective-permute-start | bytes 1966088 | tf_op jit(solution)/shard_map/ppermute | solution.py:22
  69.5 2.1 collective-permute-start.12
  71.9 15.4 %collective-permute-done.12 = bf16[128,2560]{1,0:T(8,128)(2,1)S(1)} collective-permute-done((bf16[128,2560]{1,0:T(8,128)(2,1)S(1)}, bf16[128,2560]{1,0:T(8,128)(2,1)S(1)}, u32[]{:S(2)}, u32[]{:S(2)}) %collective-permute-start.12) | collective-permute-done | bytes 655392 | tf_op jit(solution)/shard_map/ppermute | solution.py:22
  87.3 4.9 collective-permute-start.13
  92.3 3.1 and_and_fusion
  95.4 7.4 %collective-permute-start = (bf16[128,512]{1,0:T(8,128)(2,1)S(1)}, bf16[128,512]{1,0:T(8,128)(2,1)S(1)}, u32[]{:S(2)}, u32[]{:S(2)}) collective-permute-start(bf16[128,512]{1,0:T(8,128)(2,1)S(1)} %bitcast.384), channel_id=1, source_target_pairs={{0,44},{4,48},{8,52},{12,56},{16,60},{20,64},{24,68},{28,72},{32,7... | collective-permute-start | bytes 393224 | tf_op jit(solution)/shard_map/ppermute | solution.py:28
  102.8 17.8 %collective-permute-done.13 = bf16[128,2560]{1,0:T(8,128)(2,1)S(1)} collective-permute-done((bf16[128,2560]{1,0:T(8,128)(2,1)S(1)}, bf16[128,2560]{1,0:T(8,128)(2,1)S(1)}, u32[]{:S(2)}, u32[]{:S(2)}) %collective-permute-start.13) | collective-permute-done | bytes 655392 | tf_op jit(solution)/shard_map/ppermute | solution.py:22
  120.6 9.4 %collective-permute-start.14 = (bf16[128,2560]{1,0:T(8,128)(2,1)S(1)}, bf16[128,2560]{1,0:T(8,128)(2,1)S(1)}, u32[]{:S(2)}, u32[]{:S(2)}) collective-permute-start(bf16[128,2560]{1,0:T(8,128)(2,1)S(1)} %collective-permute-done.13), channel_id=1, source_target_pairs={{0,32},{32,0},{4,36},{36,4},{8,40},{40,8},{12,44},{44,12},{16,48},... | collective-permute-start | bytes 1966088 | tf_op jit(solution)/shard_map/ppermute | solution.py:22
  131.9 44.8 %collective-permute-start.2 = (bf16[128,512]{1,0:T(8,128)(2,1)S(1)}, bf16[128,512]{1,0:T(8,128)(2,1)S(1)}, u32[]{:S(2)}, u32[]{:S(2)}) collective-permute-start(bf16[128,512]{1,0:T(8,128)(2,1)S(1)} %bitcast.386), channel_id=1, source_target_pairs={{0,36},{4,40},{8,44},{12,48},{16,52},{20,56},{24,60},{28,64},{32,6... | collective-permute-start | bytes 393224 | tf_op jit(solution)/shard_map/ppermute | solution.py:28
  178.4 5.2 collective-permute-start.4
  185.2 4.0 collective-permute-done.2
  190.5 7.6 %collective-permute-start.15 = (bf16[128,2560]{1,0:T(8,128)(2,1)S(1)}, bf16[128,2560]{1,0:T(8,128)(2,1)S(1)}, u32[]{:S(2)}, u32[]{:S(2)}) collective-permute-start(bf16[128,2560]{1,0:T(8,128)(2,1)S(1)} %collective-permute-done.14), channel_id=1, source_target_pairs={{0,64},{64,0},{4,68},{68,4},{8,72},{72,8},{12,76},{76,12},{16,80},... | collective-permute-start | bytes 1966088 | tf_op jit(solution)/shard_map/ppermute | solution.py:22
  198.2 10.1 %collective-permute-start.7 = (bf16[128,512]{1,0:T(8,128)(2,1)S(1)}, bf16[128,512]{1,0:T(8,128)(2,1)S(1)}, u32[]{:S(2)}, u32[]{:S(2)}) collective-permute-start(bf16[128,512]{1,0:T(8,128)(2,1)S(1)} %bitcast.391), channel_id=1, source_target_pairs={{0,16},{4,20},{8,24},{12,28},{16,32},{20,36},{24,40},{28,44},{32,4... | collective-permute-start | bytes 393224 | tf_op jit(solution)/shard_map/ppermute | solution.py:28
  208.4 27.9 %collective-permute-start.8 = (bf16[128,512]{1,0:T(8,128)(2,1)S(1)}, bf16[128,512]{1,0:T(8,128)(2,1)S(1)}, u32[]{:S(2)}, u32[]{:S(2)}) collective-permute-start(bf16[128,512]{1,0:T(8,128)(2,1)S(1)} %bitcast.392), channel_id=1, source_target_pairs={{0,12},{4,16},{8,20},{12,24},{16,28},{20,32},{24,36},{28,40},{32,4... | collective-permute-start | bytes 393224 | tf_op jit(solution)/shard_map/ppermute | solution.py:28
  239.6 3.1 collective-permute-start.10
  242.8 24.1 %collective-permute-done.16 = bf16[128,2560]{1,0:T(8,128)(2,1)S(1)} collective-permute-done((bf16[128,2560]{1,0:T(8,128)(2,1)S(1)}, bf16[128,2560]{1,0:T(8,128)(2,1)S(1)}, u32[]{:S(2)}, u32[]{:S(2)}) %collective-permute-start.16) | collective-permute-done | bytes 655392 | tf_op jit(solution)/shard_map/ppermute | solution.py:22
  266.9 6.3 collective-permute-start.17
  273.3 29.4 %collective-permute-done.17 = bf16[128,2560]{1,0:T(8,128)(2,1)S(1)} collective-permute-done((bf16[128,2560]{1,0:T(8,128)(2,1)S(1)}, bf16[128,2560]{1,0:T(8,128)(2,1)S(1)}, u32[]{:S(2)}, u32[]{:S(2)}) %collective-permute-start.17) | collective-permute-done | bytes 655392 | tf_op jit(solution)/shard_map/ppermute | solution.py:22
  302.9 3.2 collective-permute-start.18
  318.7 64.5 %collective-permute-done.20 = bf16[2,128,512]{2,1,0:T(8,128)(2,1)S(1)} collective-permute-done((bf16[2,128,512]{2,1,0:T(8,128)(2,1)S(1)}, bf16[2,128,512]{2,1,0:T(8,128)(2,1)S(1)}, u32[]{:S(2)}, u32[]{:S(2)}) %collective-permute-start.20) | collective-permute-done | bytes 262176 | tf_op jit(solution)/shard_map/ppermute | solution.py:28
  385.2 31.7 %collective-permute-done.21 = bf16[2,128,512]{2,1,0:T(8,128)(2,1)S(1)} collective-permute-done((bf16[2,128,512]{2,1,0:T(8,128)(2,1)S(1)}, bf16[2,128,512]{2,1,0:T(8,128)(2,1)S(1)}, u32[]{:S(2)}, u32[]{:S(2)}) %collective-permute-start.21) | collective-permute-done | bytes 262176 | tf_op jit(solution)/shard_map/ppermute | solution.py:28
  424.3 20.7 %collective-permute-done.26 = bf16[2,128,512]{2,1,0:T(8,128)(2,1)S(1)} collective-permute-done((bf16[2,128,512]{2,1,0:T(8,128)(2,1)S(1)}, bf16[2,128,512]{2,1,0:T(8,128)(2,1)S(1)}, u32[]{:S(2)}, u32[]{:S(2)}) %collective-permute-start.26) | collective-permute-done | bytes 262176 | tf_op jit(solution)/shard_map/ppermute | solution.py:28
  446.6 3.0 collective-permute-done.28
  451.0 2.5 gather_fusion.1
  453.5 2.6 fusion.48
  456.1 2.6 fusion.222
  469.4 12.2 %collective-permute-start.29 = (bf16[128,2048]{1,0:T(8,128)(2,1)S(1)}, bf16[128,2048]{1,0:T(8,128)(2,1)S(1)}, u32[]{:S(2)}, u32[]{:S(2)}) collective-permute-start(bf16[128,2048]{1,0:T(8,128)(2,1)S(1)} %pad_maximum_fusion.2), channel_id=1, source_target_pairs={{0,4},{4,0},{8,12},{12,8},{16,20},{20,16},{24,28},{28,24},{32,36},... | collective-permute-start | bytes 1572872 | tf_op jit(solution)/shard_map/ppermute | solution.py:22
  483.1 11.1 %collective-permute-start.30 = (bf16[128,2048]{1,0:T(8,128)(2,1)S(1)}, bf16[128,2048]{1,0:T(8,128)(2,1)S(1)}, u32[]{:S(2)}, u32[]{:S(2)}) collective-permute-start(bf16[128,2048]{1,0:T(8,128)(2,1)S(1)} %collective-permute-done.29), channel_id=1, source_target_pairs={{0,8},{8,0},{4,12},{12,4},{16,24},{24,16},{20,28},{28,20},{32,40},... | collective-permute-start | bytes 1572872 | tf_op jit(solution)/shard_map/ppermute | solution.py:22
  494.2 12.1 %collective-permute-done.30 = bf16[128,2048]{1,0:T(8,128)(2,1)S(1)} collective-permute-done((bf16[128,2048]{1,0:T(8,128)(2,1)S(1)}, bf16[128,2048]{1,0:T(8,128)(2,1)S(1)}, u32[]{:S(2)}, u32[]{:S(2)}) %collective-permute-start.30) | collective-permute-done | bytes 524320 | tf_op jit(solution)/shard_map/ppermute | solution.py:22
  506.3 3.1 collective-permute-start.31
  510.0 23.4 %collective-permute-done.31 = bf16[128,2048]{1,0:T(8,128)(2,1)} collective-permute-done((bf16[128,2048]{1,0:T(8,128)(2,1)S(1)}, bf16[128,2048]{1,0:T(8,128)(2,1)}, u32[]{:S(2)}, u32[]{:S(2)}) %collective-permute-start.31) | collective-permute-done | bytes 524320 | tf_op jit(solution)/shard_map/ppermute | solution.py:22
  535.3 2.5 fusion.226
  539.5 20.3 %collective-permute-done.32 = bf16[128,2048]{1,0:T(8,128)(2,1)} collective-permute-done((bf16[128,2048]{1,0:T(8,128)(2,1)}, bf16[128,2048]{1,0:T(8,128)(2,1)}, u32[]{:S(2)}, u32[]{:S(2)}) %collective-permute-start.32) | collective-permute-done | bytes 524320 | tf_op jit(solution)/shard_map/ppermute | solution.py:22
  564.8 8.1 %collective-permute-done.33 = bf16[128,2048]{1,0:T(8,128)(2,1)} collective-permute-done((bf16[128,2048]{1,0:T(8,128)(2,1)}, bf16[128,2048]{1,0:T(8,128)(2,1)}, u32[]{:S(2)}, u32[]{:S(2)}) %collective-permute-start.33) | collective-permute-done | bytes 524320 | tf_op jit(solution)/shard_map/ppermute | solution.py:22
  573.0 34.7 %collective-permute-start.34 = (bf16[128,2048]{1,0:T(8,128)(2,1)}, bf16[128,2048]{1,0:T(8,128)(2,1)}, u32[]{:S(2)}, u32[]{:S(2)}) collective-permute-start(bf16[128,2048]{1,0:T(8,128)(2,1)} %collective-permute-done.33), channel_id=1, source_target_pairs={{0,128},{128,0},{4,132},{132,4},{8,136},{136,8},{12,140},{140,12},... | collective-permute-start | bytes 1572872 | tf_op jit(solution)/shard_map/ppermute | solution.py:22
  610.8 19.8 %collective-permute-done.34 = bf16[128,2048]{1,0:T(8,128)(2,1)} collective-permute-done((bf16[128,2048]{1,0:T(8,128)(2,1)}, bf16[128,2048]{1,0:T(8,128)(2,1)}, u32[]{:S(2)}, u32[]{:S(2)}) %collective-permute-start.34) | collective-permute-done | bytes 524320 | tf_op jit(solution)/shard_map/ppermute | solution.py:22
  630.6 2.2 collective-permute-start.35
  635.8 21.7 %collective-permute-done.35 = bf16[128,2048]{1,0:T(8,128)(2,1)S(1)} collective-permute-done((bf16[128,2048]{1,0:T(8,128)(2,1)}, bf16[128,2048]{1,0:T(8,128)(2,1)S(1)}, u32[]{:S(2)}, u32[]{:S(2)}) %collective-permute-start.35) | collective-permute-done | bytes 524320 | tf_op jit(solution)/shard_map/ppermute | solution.py:22
  658.6 15.1 %all_to_all.69 = bf16[2,128,2048]{2,0,1:T(2,128)(2,1)S(1)} all-to-all(bf16[2,128,2048]{2,0,1:T(2,128)(2,1)S(1)} %copy.317), channel_id=1, replica_groups=mesh['ctx'=128,'head'=4] {'head'}, dimensions={1} | all-to-all | bytes 2097152 | tf_op jit(solution)/shard_map/all_to_all | solution.py:133
  (161 shorter events, 74.9 us)
Async XLA Ops:
  0.0 15.5 %copy-start.2 = (bf16[2,32,8192]{2,1,0:T(8,128)(2,1)S(1)}, bf16[2,32,8192]{2,1,0:T(8,128)(2,1)}, u32[]{:S(2)}) copy-start(bf16[2,32,8192]{2,1,0:T(8,128)(2,1)} %param.4) | copy-start | bytes 3145732
  2.5 9.7 %all-to-all-start = ((bf16[4,2,8192]{2,1,0:T(2,128)(2,1)}), bf16[4,2,8192]{2,1,0:T(2,128)(2,1)S(1)}, u32[]{:S(2)}, u32[]{:S(2)}) async-start(bf16[4,2,8192]{2,1,0:T(2,128)(2,1)} %reshape.434), calls=%async_computation | async-start | bytes 262144 | tf_op jit(solution)/shard_map/all_to_all | solution.py:88
  12.1 16.6 %all-to-all-start.1 = ((bf16[4,2,8192]{2,1,0:T(2,128)(2,1)}), bf16[4,2,8192]{2,1,0:T(2,128)(2,1)S(1)}, u32[]{:S(2)}, u32[]{:S(2)}) async-start(bf16[4,2,8192]{2,1,0:T(2,128)(2,1)} %reshape.436), calls=%async_computation.1 | async-start | bytes 262144 | tf_op jit(solution)/shard_map/all_to_all | solution.py:89
  22.3 10.6 %copy-start.11 = (s32[47]{0:T(128)S(1)}, s32[47]{0:T(128)}, u32[]{:S(2)}) copy-start(s32[47]{0:T(128)} %param.7) | copy-start | bytes 568
  28.7 13.9 %all-to-all-start.2 = ((bf16[4,2,65536]{2,1,0:T(2,128)(2,1)}), bf16[4,2,65536]{2,1,0:T(2,128)(2,1)S(1)}, u32[]{:S(2)}, u32[]{:S(2)}) async-start(bf16[4,2,65536]{2,1,0:T(2,128)(2,1)} %reshape.438), calls=%async_computation.2 | async-start | bytes 2097152 | tf_op jit(solution)/shard_map/all_to_all | solution.py:87
  57.7 11.8 %collective-permute-start.11 = (bf16[128,2560]{1,0:T(8,128)(2,1)S(1)}, bf16[128,2560]{1,0:T(8,128)(2,1)S(1)}, u32[]{:S(2)}, u32[]{:S(2)}) collective-permute-start(bf16[128,2560]{1,0:T(8,128)(2,1)S(1)} %pad_maximum_fusion.1), channel_id=1, source_target_pairs={{0,4},{4,0},{8,12},{12,8},{16,20},{20,16},{24,28},{28,24},{32,36},... | collective-permute-start | bytes 1966088 | tf_op jit(solution)/shard_map/ppermute | solution.py:22
  69.5 17.8 %collective-permute-start.12 = (bf16[128,2560]{1,0:T(8,128)(2,1)S(1)}, bf16[128,2560]{1,0:T(8,128)(2,1)S(1)}, u32[]{:S(2)}, u32[]{:S(2)}) collective-permute-start(bf16[128,2560]{1,0:T(8,128)(2,1)S(1)} %collective-permute-done.11), channel_id=1, source_target_pairs={{0,8},{8,0},{4,12},{12,4},{16,24},{24,16},{20,28},{28,20},{32,40},... | collective-permute-start | bytes 1966088 | tf_op jit(solution)/shard_map/ppermute | solution.py:22
  87.3 33.2 %collective-permute-start.13 = (bf16[128,2560]{1,0:T(8,128)(2,1)S(1)}, bf16[128,2560]{1,0:T(8,128)(2,1)S(1)}, u32[]{:S(2)}, u32[]{:S(2)}) collective-permute-start(bf16[128,2560]{1,0:T(8,128)(2,1)S(1)} %collective-permute-done.12), channel_id=1, source_target_pairs={{0,16},{16,0},{4,20},{20,4},{8,24},{24,8},{12,28},{28,12},{32,48},... | collective-permute-start | bytes 1966088 | tf_op jit(solution)/shard_map/ppermute | solution.py:22
  95.4 83.0 %collective-permute-start = (bf16[128,512]{1,0:T(8,128)(2,1)S(1)}, bf16[128,512]{1,0:T(8,128)(2,1)S(1)}, u32[]{:S(2)}, u32[]{:S(2)}) collective-permute-start(bf16[128,512]{1,0:T(8,128)(2,1)S(1)} %bitcast.384), channel_id=1, source_target_pairs={{0,44},{4,48},{8,52},{12,56},{16,60},{20,64},{24,68},{28,72},{32,7... | collective-permute-start | bytes 393224 | tf_op jit(solution)/shard_map/ppermute | solution.py:28
  120.6 70.0 %collective-permute-start.14 = (bf16[128,2560]{1,0:T(8,128)(2,1)S(1)}, bf16[128,2560]{1,0:T(8,128)(2,1)S(1)}, u32[]{:S(2)}, u32[]{:S(2)}) collective-permute-start(bf16[128,2560]{1,0:T(8,128)(2,1)S(1)} %collective-permute-done.13), channel_id=1, source_target_pairs={{0,32},{32,0},{4,36},{36,4},{8,40},{40,8},{12,44},{44,12},{16,48},... | collective-permute-start | bytes 1966088 | tf_op jit(solution)/shard_map/ppermute | solution.py:22
  130.6 53.0 %collective-permute-start.1 = (bf16[128,512]{1,0:T(8,128)(2,1)S(1)}, bf16[128,512]{1,0:T(8,128)(2,1)S(1)}, u32[]{:S(2)}, u32[]{:S(2)}) collective-permute-start(bf16[128,512]{1,0:T(8,128)(2,1)S(1)} %bitcast.385), channel_id=1, source_target_pairs={{0,40},{4,44},{8,48},{12,52},{16,56},{20,60},{24,64},{28,68},{32,7... | collective-permute-start | bytes 393224 | tf_op jit(solution)/shard_map/ppermute | solution.py:28
  131.9 57.4 %collective-permute-start.2 = (bf16[128,512]{1,0:T(8,128)(2,1)S(1)}, bf16[128,512]{1,0:T(8,128)(2,1)S(1)}, u32[]{:S(2)}, u32[]{:S(2)}) collective-permute-start(bf16[128,512]{1,0:T(8,128)(2,1)S(1)} %bitcast.386), channel_id=1, source_target_pairs={{0,36},{4,40},{8,44},{12,48},{16,52},{20,56},{24,60},{28,64},{32,6... | collective-permute-start | bytes 393224 | tf_op jit(solution)/shard_map/ppermute | solution.py:28
  176.7 21.5 %collective-permute-start.3 = (bf16[128,512]{1,0:T(8,128)(2,1)S(1)}, bf16[128,512]{1,0:T(8,128)(2,1)S(1)}, u32[]{:S(2)}, u32[]{:S(2)}) collective-permute-start(bf16[128,512]{1,0:T(8,128)(2,1)S(1)} %bitcast.387), channel_id=1, source_target_pairs={{0,32},{4,36},{8,40},{12,44},{16,48},{20,52},{24,56},{28,60},{32,6... | collective-permute-start | bytes 393224 | tf_op jit(solution)/shard_map/ppermute | solution.py:28
  178.4 30.0 %collective-permute-start.4 = (bf16[128,512]{1,0:T(8,128)(2,1)S(1)}, bf16[128,512]{1,0:T(8,128)(2,1)S(1)}, u32[]{:S(2)}, u32[]{:S(2)}) collective-permute-start(bf16[128,512]{1,0:T(8,128)(2,1)S(1)} %bitcast.388), channel_id=1, source_target_pairs={{0,28},{4,32},{8,36},{12,40},{16,44},{20,48},{24,52},{28,56},{32,6... | collective-permute-start | bytes 393224 | tf_op jit(solution)/shard_map/ppermute | solution.py:28
  183.6 52.7 %collective-permute-start.5 = (bf16[128,512]{1,0:T(8,128)(2,1)S(1)}, bf16[128,512]{1,0:T(8,128)(2,1)S(1)}, u32[]{:S(2)}, u32[]{:S(2)}) collective-permute-start(bf16[128,512]{1,0:T(8,128)(2,1)S(1)} %bitcast.389), channel_id=1, source_target_pairs={{0,24},{4,28},{8,32},{12,36},{16,40},{20,44},{24,48},{28,52},{32,5... | collective-permute-start | bytes 393224 | tf_op jit(solution)/shard_map/ppermute | solution.py:28
  189.2 50.3 %collective-permute-start.6 = (bf16[128,512]{1,0:T(8,128)(2,1)S(1)}, bf16[128,512]{1,0:T(8,128)(2,1)S(1)}, u32[]{:S(2)}, u32[]{:S(2)}) collective-permute-start(bf16[128,512]{1,0:T(8,128)(2,1)S(1)} %bitcast.390), channel_id=1, source_target_pairs={{0,20},{4,24},{8,28},{12,32},{16,36},{20,40},{24,44},{28,48},{32,5... | collective-permute-start | bytes 393224 | tf_op jit(solution)/shard_map/ppermute | solution.py:28
  190.5 47.1 %collective-permute-start.15 = (bf16[128,2560]{1,0:T(8,128)(2,1)S(1)}, bf16[128,2560]{1,0:T(8,128)(2,1)S(1)}, u32[]{:S(2)}, u32[]{:S(2)}) collective-permute-start(bf16[128,2560]{1,0:T(8,128)(2,1)S(1)} %collective-permute-done.14), channel_id=1, source_target_pairs={{0,64},{64,0},{4,68},{68,4},{8,72},{72,8},{12,76},{76,12},{16,80},... | collective-permute-start | bytes 1966088 | tf_op jit(solution)/shard_map/ppermute | solution.py:22
  198.2 44.5 %collective-permute-start.7 = (bf16[128,512]{1,0:T(8,128)(2,1)S(1)}, bf16[128,512]{1,0:T(8,128)(2,1)S(1)}, u32[]{:S(2)}, u32[]{:S(2)}) collective-permute-start(bf16[128,512]{1,0:T(8,128)(2,1)S(1)} %bitcast.391), channel_id=1, source_target_pairs={{0,16},{4,20},{8,24},{12,28},{16,32},{20,36},{24,40},{28,44},{32,4... | collective-permute-start | bytes 393224 | tf_op jit(solution)/shard_map/ppermute | solution.py:28
  208.4 64.8 %collective-permute-start.8 = (bf16[128,512]{1,0:T(8,128)(2,1)S(1)}, bf16[128,512]{1,0:T(8,128)(2,1)S(1)}, u32[]{:S(2)}, u32[]{:S(2)}) collective-permute-start(bf16[128,512]{1,0:T(8,128)(2,1)S(1)} %bitcast.392), channel_id=1, source_target_pairs={{0,12},{4,16},{8,20},{12,24},{16,28},{20,32},{24,36},{28,40},{32,4... | collective-permute-start | bytes 393224 | tf_op jit(solution)/shard_map/ppermute | solution.py:28
  236.3 37.0 %collective-permute-start.9 = (bf16[128,512]{1,0:T(8,128)(2,1)S(1)}, bf16[128,512]{1,0:T(8,128)(2,1)S(1)}, u32[]{:S(2)}, u32[]{:S(2)}) collective-permute-start(bf16[128,512]{1,0:T(8,128)(2,1)S(1)} %bitcast.393), channel_id=1, source_target_pairs={{0,8},{4,12},{8,16},{12,20},{16,24},{20,28},{24,32},{28,36},{32,40... | collective-permute-start | bytes 393224 | tf_op jit(solution)/shard_map/ppermute | solution.py:28
  237.6 29.3 %collective-permute-start.16 = (bf16[128,2560]{1,0:T(8,128)(2,1)S(1)}, bf16[128,2560]{1,0:T(8,128)(2,1)S(1)}, u32[]{:S(2)}, u32[]{:S(2)}) collective-permute-start(bf16[128,2560]{1,0:T(8,128)(2,1)S(1)} %collective-permute-done.15), channel_id=1, source_target_pairs={{0,128},{128,0},{4,132},{132,4},{8,136},{136,8},{12,140},{140,12},... | collective-permute-start | bytes 1966088 | tf_op jit(solution)/shard_map/ppermute | solution.py:22
  239.6 33.7 %collective-permute-start.10 = (bf16[128,512]{1,0:T(8,128)(2,1)S(1)}, bf16[128,512]{1,0:T(8,128)(2,1)S(1)}, u32[]{:S(2)}, u32[]{:S(2)}) collective-permute-start(bf16[128,512]{1,0:T(8,128)(2,1)S(1)} %bitcast.394), channel_id=1, source_target_pairs={{0,4},{4,8},{8,12},{12,16},{16,20},{20,24},{24,28},{28,32},{32,36}... | collective-permute-start | bytes 393224 | tf_op jit(solution)/shard_map/ppermute | solution.py:28
  266.9 35.9 %collective-permute-start.17 = (bf16[128,2560]{1,0:T(8,128)(2,1)S(1)}, bf16[128,2560]{1,0:T(8,128)(2,1)S(1)}, u32[]{:S(2)}, u32[]{:S(2)}) collective-permute-start(bf16[128,2560]{1,0:T(8,128)(2,1)S(1)} %collective-permute-done.16), channel_id=1, source_target_pairs={{0,256},{256,0},{4,260},{260,4},{8,264},{264,8},{12,268},{268,12},... | collective-permute-start | bytes 1966088 | tf_op jit(solution)/shard_map/ppermute | solution.py:22
  302.9 10.9 %collective-permute-start.18 = (bf16[2,128,512]{2,1,0:T(8,128)(2,1)S(1)}, bf16[2,128,512]{2,1,0:T(8,128)(2,1)}, u32[]{:S(2)}, u32[]{:S(2)}) collective-permute-start(bf16[2,128,512]{2,1,0:T(8,128)(2,1)S(1)} %pad_maximum_fusion.3), channel_id=1, source_target_pairs={{4,0},{8,4},{12,8},{16,12},{20,16},{24,20},{28,24},{32,28},{36,32}... | collective-permute-start | bytes 786440 | tf_op jit(solution)/shard_map/ppermute | solution.py:28
  306.1 3.9 copy-start.3
  306.1 5.2 copy-start.9
  306.1 10.6 %collective-permute-start.19 = (bf16[2,128,512]{2,1,0:T(8,128)(2,1)S(1)}, bf16[2,128,512]{2,1,0:T(8,128)(2,1)S(1)}, u32[]{:S(2)}, u32[]{:S(2)}) collective-permute-start(bf16[2,128,512]{2,1,0:T(8,128)(2,1)S(1)} %pad_maximum_fusion.3), channel_id=1, source_target_pairs={{8,0},{12,4},{16,8},{20,12},{24,16},{28,20},{32,24},{36,28},{40,32... | collective-permute-start | bytes 786440 | tf_op jit(solution)/shard_map/ppermute | solution.py:28
  307.4 75.8 %collective-permute-start.20 = (bf16[2,128,512]{2,1,0:T(8,128)(2,1)S(1)}, bf16[2,128,512]{2,1,0:T(8,128)(2,1)S(1)}, u32[]{:S(2)}, u32[]{:S(2)}) collective-permute-start(bf16[2,128,512]{2,1,0:T(8,128)(2,1)S(1)} %pad_maximum_fusion.3), channel_id=1, source_target_pairs={{12,0},{16,4},{20,8},{24,12},{28,16},{32,20},{36,24},{40,28},{44,3... | collective-permute-start | bytes 786440 | tf_op jit(solution)/shard_map/ppermute | solution.py:28
  308.7 108.1 %collective-permute-start.21 = (bf16[2,128,512]{2,1,0:T(8,128)(2,1)S(1)}, bf16[2,128,512]{2,1,0:T(8,128)(2,1)S(1)}, u32[]{:S(2)}, u32[]{:S(2)}) collective-permute-start(bf16[2,128,512]{2,1,0:T(8,128)(2,1)S(1)} %pad_maximum_fusion.3), channel_id=1, source_target_pairs={{16,0},{20,4},{24,8},{28,12},{32,16},{36,20},{40,24},{44,28},{48,3... | collective-permute-start | bytes 786440 | tf_op jit(solution)/shard_map/ppermute | solution.py:28
  310.0 108.8 %collective-permute-start.22 = (bf16[2,128,512]{2,1,0:T(8,128)(2,1)S(1)}, bf16[2,128,512]{2,1,0:T(8,128)(2,1)S(1)}, u32[]{:S(2)}, u32[]{:S(2)}) collective-permute-start(bf16[2,128,512]{2,1,0:T(8,128)(2,1)S(1)} %pad_maximum_fusion.3), channel_id=1, source_target_pairs={{20,0},{24,4},{28,8},{32,12},{36,16},{40,20},{44,24},{48,28},{52,3... | collective-permute-start | bytes 786440 | tf_op jit(solution)/shard_map/ppermute | solution.py:28
  313.8 107.0 %collective-permute-start.23 = (bf16[2,128,512]{2,1,0:T(8,128)(2,1)S(1)}, bf16[2,128,512]{2,1,0:T(8,128)(2,1)S(1)}, u32[]{:S(2)}, u32[]{:S(2)}) collective-permute-start(bf16[2,128,512]{2,1,0:T(8,128)(2,1)S(1)} %pad_maximum_fusion.3), channel_id=1, source_target_pairs={{24,0},{28,4},{32,8},{36,12},{40,16},{44,20},{48,24},{52,28},{56,3... | collective-permute-start | bytes 786440 | tf_op jit(solution)/shard_map/ppermute | solution.py:28
  316.7 106.2 %collective-permute-start.24 = (bf16[2,128,512]{2,1,0:T(8,128)(2,1)S(1)}, bf16[2,128,512]{2,1,0:T(8,128)(2,1)S(1)}, u32[]{:S(2)}, u32[]{:S(2)}) collective-permute-start(bf16[2,128,512]{2,1,0:T(8,128)(2,1)S(1)} %pad_maximum_fusion.3), channel_id=1, source_target_pairs={{28,0},{32,4},{36,8},{40,12},{44,16},{48,20},{52,24},{56,28},{60,3... | collective-permute-start | bytes 786440 | tf_op jit(solution)/shard_map/ppermute | solution.py:28
  383.2 40.4 %collective-permute-start.25 = (bf16[2,128,512]{2,1,0:T(8,128)(2,1)S(1)}, bf16[2,128,512]{2,1,0:T(8,128)(2,1)S(1)}, u32[]{:S(2)}, u32[]{:S(2)}) collective-permute-start(bf16[2,128,512]{2,1,0:T(8,128)(2,1)S(1)} %pad_maximum_fusion.3), channel_id=1, source_target_pairs={{32,0},{36,4},{40,8},{44,12},{48,16},{52,20},{56,24},{60,28},{64,3... | collective-permute-start | bytes 786440 | tf_op jit(solution)/shard_map/ppermute | solution.py:28
  416.9 28.1 %collective-permute-start.26 = (bf16[2,128,512]{2,1,0:T(8,128)(2,1)S(1)}, bf16[2,128,512]{2,1,0:T(8,128)(2,1)S(1)}, u32[]{:S(2)}, u32[]{:S(2)}) collective-permute-start(bf16[2,128,512]{2,1,0:T(8,128)(2,1)S(1)} %pad_maximum_fusion.3), channel_id=1, source_target_pairs={{36,0},{40,4},{44,8},{48,12},{52,16},{56,20},{60,24},{64,28},{68,3... | collective-permute-start | bytes 786440 | tf_op jit(solution)/shard_map/ppermute | solution.py:28
  418.8 27.1 %collective-permute-start.27 = (bf16[2,128,512]{2,1,0:T(8,128)(2,1)S(1)}, bf16[2,128,512]{2,1,0:T(8,128)(2,1)S(1)}, u32[]{:S(2)}, u32[]{:S(2)}) collective-permute-start(bf16[2,128,512]{2,1,0:T(8,128)(2,1)S(1)} %pad_maximum_fusion.3), channel_id=1, source_target_pairs={{40,0},{44,4},{48,8},{52,12},{56,16},{60,20},{64,24},{68,28},{72,3... | collective-permute-start | bytes 786440 | tf_op jit(solution)/shard_map/ppermute | solution.py:28
  420.8 28.8 %collective-permute-start.28 = (bf16[2,128,512]{2,1,0:T(8,128)(2,1)S(1)}, bf16[2,128,512]{2,1,0:T(8,128)(2,1)S(1)}, u32[]{:S(2)}, u32[]{:S(2)}) collective-permute-start(bf16[2,128,512]{2,1,0:T(8,128)(2,1)S(1)} %pad_maximum_fusion.3), channel_id=1, source_target_pairs={{44,0},{48,4},{52,8},{56,12},{60,16},{64,20},{68,24},{72,28},{76,3... | collective-permute-start | bytes 786440 | tf_op jit(solution)/shard_map/ppermute | solution.py:28
  453.5 2.6 copy-start.5
  456.1 2.6 copy-start.1
  456.1 2.6 copy-start.8
  467.7 41.8 %copy-start = (bf16[1,4,32,2048]{3,1,2,0:T(4,128)(2,1)S(1)}, bf16[1,4,32,2048]{3,1,2,0:T(4,128)(2,1)}, u32[]{:S(2)}) copy-start(bf16[1,4,32,2048]{3,1,2,0:T(4,128)(2,1)} %get-tuple-element.9) | copy-start | bytes 1572868
  469.2 66.1 %copy-start.4 = (pred[128,1536]{0,1:T(8,128)(4,1)S(1)}, pred[128,1536]{0,1:T(8,128)(4,1)}, u32[]{:S(2)}) copy-start(pred[128,1536]{0,1:T(8,128)(4,1)} %get-tuple-element.73) | copy-start | bytes 589828
  469.4 13.7 %collective-permute-start.29 = (bf16[128,2048]{1,0:T(8,128)(2,1)S(1)}, bf16[128,2048]{1,0:T(8,128)(2,1)S(1)}, u32[]{:S(2)}, u32[]{:S(2)}) collective-permute-start(bf16[128,2048]{1,0:T(8,128)(2,1)S(1)} %pad_maximum_fusion.2), channel_id=1, source_target_pairs={{0,4},{4,0},{8,12},{12,8},{16,20},{20,16},{24,28},{28,24},{32,36},... | collective-permute-start | bytes 1572872 | tf_op jit(solution)/shard_map/ppermute | solution.py:22
  483.1 23.3 %collective-permute-start.30 = (bf16[128,2048]{1,0:T(8,128)(2,1)S(1)}, bf16[128,2048]{1,0:T(8,128)(2,1)S(1)}, u32[]{:S(2)}, u32[]{:S(2)}) collective-permute-start(bf16[128,2048]{1,0:T(8,128)(2,1)S(1)} %collective-permute-done.29), channel_id=1, source_target_pairs={{0,8},{8,0},{4,12},{12,4},{16,24},{24,16},{20,28},{28,20},{32,40},... | collective-permute-start | bytes 1572872 | tf_op jit(solution)/shard_map/ppermute | solution.py:22
  506.3 27.0 %collective-permute-start.31 = (bf16[128,2048]{1,0:T(8,128)(2,1)S(1)}, bf16[128,2048]{1,0:T(8,128)(2,1)}, u32[]{:S(2)}, u32[]{:S(2)}) collective-permute-start(bf16[128,2048]{1,0:T(8,128)(2,1)S(1)} %collective-permute-done.30), channel_id=1, source_target_pairs={{0,16},{16,0},{4,20},{20,4},{8,24},{24,8},{12,28},{28,12},{32,48},... | collective-permute-start | bytes 1572872 | tf_op jit(solution)/shard_map/ppermute | solution.py:22
  533.4 26.4 %collective-permute-start.32 = (bf16[128,2048]{1,0:T(8,128)(2,1)}, bf16[128,2048]{1,0:T(8,128)(2,1)}, u32[]{:S(2)}, u32[]{:S(2)}) collective-permute-start(bf16[128,2048]{1,0:T(8,128)(2,1)} %collective-permute-done.31), channel_id=1, source_target_pairs={{0,32},{32,0},{4,36},{36,4},{8,40},{40,8},{12,44},{44,12},{16,48},... | collective-permute-start | bytes 1572872 | tf_op jit(solution)/shard_map/ppermute | solution.py:22
  559.8 13.2 %collective-permute-start.33 = (bf16[128,2048]{1,0:T(8,128)(2,1)}, bf16[128,2048]{1,0:T(8,128)(2,1)}, u32[]{:S(2)}, u32[]{:S(2)}) collective-permute-start(bf16[128,2048]{1,0:T(8,128)(2,1)} %collective-permute-done.32), channel_id=1, source_target_pairs={{0,64},{64,0},{4,68},{68,4},{8,72},{72,8},{12,76},{76,12},{16,80},... | collective-permute-start | bytes 1572872 | tf_op jit(solution)/shard_map/ppermute | solution.py:22
  573.0 57.7 %collective-permute-start.34 = (bf16[128,2048]{1,0:T(8,128)(2,1)}, bf16[128,2048]{1,0:T(8,128)(2,1)}, u32[]{:S(2)}, u32[]{:S(2)}) collective-permute-start(bf16[128,2048]{1,0:T(8,128)(2,1)} %collective-permute-done.33), channel_id=1, source_target_pairs={{0,128},{128,0},{4,132},{132,4},{8,136},{136,8},{12,140},{140,12},... | collective-permute-start | bytes 1572872 | tf_op jit(solution)/shard_map/ppermute | solution.py:22
  630.6 26.8 %collective-permute-start.35 = (bf16[128,2048]{1,0:T(8,128)(2,1)}, bf16[128,2048]{1,0:T(8,128)(2,1)S(1)}, u32[]{:S(2)}, u32[]{:S(2)}) collective-permute-start(bf16[128,2048]{1,0:T(8,128)(2,1)} %collective-permute-done.34), channel_id=1, source_target_pairs={{0,256},{256,0},{4,260},{260,4},{8,264},{264,8},{12,268},{268,12},... | collective-permute-start | bytes 1572872 | tf_op jit(solution)/shard_map/ppermute | solution.py:22
  (3 other events, 5.7 us)
where the time goes:
time: 682 us; the launch traced here: 675 us
  waiting for transfers between devices  330 us (48%)
  starting transfers between devices  244 us (36%)
  local copies, waits for them, and re-layouts  53.2 us (8%)
  matrix products  25.2 us (4%)
  blocking collectives  15.1 us (2%)
  other arithmetic  7.01 us (1%)
    ppermute x14, waiting for transfers between devices, partner(): return lax.ppermute(block, axis, route)  195 us
    ppermute x22, waiting for transfers between devices, shifted(): return lax.ppermute(block, axis, route)  124 us
    ppermute x22, starting transfers between devices, shifted(): return lax.ppermute(block, axis, route)  122 us
    ppermute x14, starting transfers between devices, partner(): return lax.ppermute(block, axis, route)  109 us
    unnamed x55, local copies, waits for them, and re-layouts  30 us
    all_to_all x1, blocking collectives, per_device(): lax.all_to_all(result, 'head', split_axis=1, concat_axis=2, tiled=True)  15.1 us
  transfers between devices with their start and end apart: 39, of which 20 were waited for; matrix products, arithmetic and copies ran while one was open for 7% of the time, Pallas kernels for 0%

commit v1 on v0

v1 whole, which is shorter than its diff:
```python
import functools
import math

import jax
import jax.numpy as jnp
from jax import lax
from jax.experimental import pallas as pl
from jax.experimental.pallas import tpu as pltpu
from jax.sharding import PartitionSpec as P

MESH = pl.DeviceIdType.MESH
HD = 128
HEADS = 8
GROUP = 8
SIDE = 4
GROUP_SIZE = 8
SLOTS = 7
NEG_FILL = -1e30
FACTOR = 1.0 / math.sqrt(HD) * math.log2(math.e)


def attention_kernel(
    rows,
    groups,
    half_len,
    q_ref,
    k_ref,
    v_ref,
    len_ref,
    out_ref,
    q_all,
    k_win,
    v_win,
    o_all,
    bias,
    scores,
    sent,
    own_sem,
    q_sem,
    up_sem,
    down_sem,
    chain_sent,
    out_sem,
):
    ctx = lax.axis_index("ctx")
    x = lax.axis_index("head")
    core = lax.rem(ctx, 2)
    group = ctx // 2
    me = core * SIDE + x
    span = rows * GROUP_SIZE
    block = span // 2
    wide = GROUP * HD
    own_row = (SLOTS - 1) * span
    window = (SLOTS - 2) * span + 2 * block

    def member(index):
        return (group * 2 + index // SIDE, lax.rem(index, SIDE))

    def along(step):
        return (lax.rem(group + step + groups, groups) * 2 + core, x)

    barrier = pltpu.get_barrier_semaphore()
    for k in range(1, GROUP_SIZE):
        other = member(lax.rem(me + k, GROUP_SIZE))
        pl.semaphore_signal(barrier, inc=1, device_id=other, device_id_type=MESH)
    for step in (1, -1, SLOTS - 1, 1 - SLOTS):
        pl.semaphore_signal(barrier, inc=1, device_id=along(step), device_id_type=MESH)
    pl.semaphore_wait(barrier, GROUP_SIZE + 3)

    my_rows = pl.ds(pl.multiple_of(own_row + me * rows, rows), rows)
    for which, (src, dst) in enumerate(((k_ref, k_win), (v_ref, v_win))):
        for half in range(2):
            for k in range(GROUP_SIZE):
                index = lax.rem(me + k, GROUP_SIZE)
                cols = pl.ds(pl.multiple_of(index * HD, HD), HD)
                if k:
                    pltpu.make_async_remote_copy(
                        src.at[half, :, cols],
                        dst.at[half, my_rows, :],
                        sent.at[which],
                        own_sem.at[which, half],
                        device_id=member(index),
                        device_id_type=MESH,
                    ).start()
                else:
                    pltpu.make_async_copy(
                        src.at[half, :, cols], dst.at[half, my_rows, :], own_sem.at[which, half]
                    ).start()

    q_rows = pl.ds(pl.multiple_of(me * rows, rows), rows)
    for half in range(2):
        for k in range(GROUP_SIZE):
            index = lax.rem(me + k, GROUP_SIZE)
            cols = pl.ds(pl.multiple_of(index * wide, wide), wide)
            if k:
                pltpu.make_async_remote_copy(
                    q_ref.at[half, :, cols],
                    q_all.at[half, q_rows, :],
                    sent.at[2],
                    q_sem.at[half],
                    device_id=member(index),
                    device_id_type=MESH,
                ).start()
            else:
                pltpu.make_async_copy(q_ref.at[half, :, cols], q_all.at[half, q_rows, :], q_sem.at[half]).start()

    def slot_rows(slot):
        return pl.ds((SLOTS - 1 - slot) * span, span)

    def hop(which, half, from_slot, to_slot, step, sem):
        ref = (k_win, v_win)[which]
        crossed = (group + step + groups) // groups - 1
        to_half = lax.rem(half + crossed + 2, 2)
        return pltpu.make_async_remote_copy(
            ref.at[half, slot_rows(from_slot), :],
            ref.at[to_half, slot_rows(to_slot), :],
            chain_sent.at[which],
            sem.at[to_half],
            device_id=along(step),
            device_id_type=MESH,
        )

    def arrived(which, half, slot, sem):
        ref = (k_win, v_win)[which].at[half, slot_rows(slot), :]
        pltpu.make_async_copy(ref, ref, sem.at[half]).wait()

    for which in range(2):
        for half in range(2):
            arrived(which, half, 0, own_sem.at[which])
            hop(which, half, 0, 1, 1, up_sem.at[0, which]).start()
            hop(which, half, 0, 6, 6, down_sem.at[0, which]).start()

    for half in range(2):
        for part in range(2):
            first = half * half_len + group * span + part * block
            pos = first + lax.broadcasted_iota(jnp.int32, (block, 1), 0)

            def one_doc(i, carry):
                end, begin = carry
                end = end + len_ref[i]
                return end, jnp.where(pos >= end, end, begin)

            _, begin = lax.fori_loop(0, len_ref.shape[0], one_doc, (jnp.int32(0), jnp.zeros((block, 1), jnp.int32)))
            key_pos = first - (window - block) + lax.broadcasted_iota(jnp.int32, (1, window), 1)
            allowed = (key_pos >= begin) & (key_pos <= pos)
            bias[half * 2 + part] = jnp.where(allowed, 0.0, NEG_FILL)

    for step in range(3):
        for which in range(2):
            for half in range(2):
                arrived(which, half, step + 1, up_sem.at[step, which])
                if step < 2 or which == 0:
                    hop(which, half, step + 1, step + 2, 1, up_sem.at[step + 1, which]).start()
                if step < 2:
                    arrived(which, half, 6 - step, down_sem.at[step, which])
                    if step == 0 or which == 1:
                        hop(which, half, 6 - step, 5 - step, -1, down_sem.at[step + 1, which]).start()

    def unit(u, half):
        part = u // 2
        side = lax.rem(u, 2)
        row0 = pl.multiple_of(part * block, block)
        col0 = pl.multiple_of(side * (wide // 2), wide // 2)
        keys_from = pl.multiple_of(block + part * block, block)
        queries = jnp.concatenate(
            [
                q_all[half, pl.ds(row0, block), pl.ds(pl.multiple_of(col0 + i * HD, HD), HD)]
                for i in range(GROUP // 2)
            ],
            axis=0,
        )
        keys = k_win[half, pl.ds(keys_from, window), :]
        for tile in range(window // 256):
            part_keys = keys[tile * 256 : (tile + 1) * 256]
            product = lax.dot_general(
                queries, part_keys, (((1,), (1,)), ((), ())), preferred_element_type=jnp.float32
            )
            add = bias[half * 2 + part, :, tile * 256 : (tile + 1) * 256]
            scores[:, tile * 256 : (tile + 1) * 256] = (
                product.reshape(GROUP // 2, block, 256) + add[None]
            ).reshape(GROUP // 2 * block, 256)
        values = v_win[half, pl.ds(keys_from, window), :]
        values = jnp.concatenate([values, jnp.ones_like(values)], axis=1)
        for i in range(GROUP // 2):
            s = scores[i * block : (i + 1) * block, :]
            top = jnp.max(s, axis=1, keepdims=True)
            weight = jnp.exp2((s - top) * FACTOR).astype(jnp.bfloat16)
            mixed = jnp.dot(weight, values, preferred_element_type=jnp.float32)
            o_all[half * 4 + u, :, i * HD : (i + 1) * HD] = (mixed[:, :HD] / mixed[:, HD:]).astype(jnp.bfloat16)
        for k in range(SIDE):
            to_x = lax.rem(x + k, SIDE)
            src = o_all.at[half * 4 + u, pl.ds(pl.multiple_of(to_x * rows, rows), rows), :]
            dst = out_ref.at[half, :, pl.ds(pl.multiple_of(me * wide + col0, wide // 2), wide // 2)]

            def remote():
                pltpu.make_async_remote_copy(
                    src,
                    dst,
                    sent.at[3],
                    out_sem,
                    device_id=(group * 2 + part, to_x),
                    device_id_type=MESH,
                ).start()

            if k:
                remote()
            else:
                pl.when(part != core)(remote)

                @pl.when(part == core)
                def _():
                    pltpu.make_async_copy(src, dst, out_sem).start()

        return 0

    for half in range(2):
        pltpu.make_async_copy(q_all.at[half], q_all.at[half], q_sem.at[half]).wait()
        arrived(0, half, 4, up_sem.at[3, 0])
        arrived(1, half, 4, down_sem.at[2, 1])
    for half in range(2):
        lax.fori_loop(0, 4, lambda u, _, half=half: unit(u, half), 0)

    pltpu.make_async_copy(out_ref, out_ref, out_sem).wait()
    others = k_ref.at[:, :, : (GROUP_SIZE - 1) * HD]
    pltpu.make_async_copy(others, others, sent.at[0]).wait()
    pltpu.make_async_copy(others, others, sent.at[1]).wait()
    others = q_ref.at[:, :, : (GROUP_SIZE - 1) * wide]
    pltpu.make_async_copy(others, others, sent.at[2]).wait()
    pltpu.make_async_copy(others, others, sent.at[3]).wait()
    for which in range(2):
        hops = (k_win, v_win)[which].at[:, pl.ds(0, 6 * span), :]
        pltpu.make_async_copy(hops, hops, chain_sent.at[which]).wait()


def per_device(queries, keys, values, doc_lengths):
    rows = queries.shape[1]
    groups = lax.axis_size("ctx") // 2
    half_len = rows * GROUP_SIZE * groups
    span = rows * GROUP_SIZE
    block = span // 2
    window = (SLOTS - 1) * span
    pairs = 2 * span * GROUP
    body = functools.partial(attention_kernel, rows, groups, half_len)
    anywhere = pl.BlockSpec(memory_space=pl.ANY)
    return pl.pallas_call(
        body,
        out_shape=jax.ShapeDtypeStruct(queries.shape, queries.dtype),
        in_specs=[anywhere, anywhere, anywhere, pl.BlockSpec(memory_space=pltpu.SMEM)],
        out_specs=anywhere,
        scratch_shapes=[
            pltpu.VMEM((2, span, GROUP * HD), jnp.bfloat16),
            pltpu.VMEM((2, SLOTS * span, HD), jnp.bfloat16),
            pltpu.VMEM((2, SLOTS * span, HD), jnp.bfloat16),
            pltpu.VMEM((8, block, GROUP // 2 * HD), jnp.bfloat16),
            pltpu.VMEM((4, block, window), jnp.float32),
            pltpu.VMEM((GROUP // 2 * block, window), jnp.float32),
            pltpu.SemaphoreType.DMA((4,)),
            pltpu.SemaphoreType.DMA((2, 2)),
            pltpu.SemaphoreType.DMA((2,)),
            pltpu.SemaphoreType.DMA((4, 2, 2)),
            pltpu.SemaphoreType.DMA((3, 2, 2)),
            pltpu.SemaphoreType.DMA((2,)),
            pltpu.SemaphoreType.DMA,
        ],
        compiler_params=pltpu.CompilerParams(
            collective_id=0, has_side_effects=True, vmem_limit_bytes=48 << 20
        ),
        cost_estimate=pl.CostEstimate(
            flops=4 * pairs * window * HD, bytes_accessed=5 << 20, transcendentals=pairs * window
        ),
    )(queries, keys, values, doc_lengths)


def solution(mesh):
    placed = P(None, ("ctx", "head"), None)
    return jax.shard_map(
        per_device,
        mesh=mesh,
        in_specs=(placed, placed, placed, P()),
        out_specs=placed,
        check_vma=False,
    )
```

time: 682 us -> 67.5 us (0.10)
  waiting for transfers between devices: 330 us -> 0 us
  starting transfers between devices: 244 us -> 0 us
  Pallas kernels: 0 us -> 62.7 us
  local copies, waits for them, and re-layouts: 53.2 us -> 4.66 us
  matrix products: 25.2 us -> 0 us
  blocking collectives: 15.1 us -> 0 us
  other arithmetic: 7.01 us -> 0 us
    ppermute x36 -> x0, waiting for transfers between devices: 320 us -> none  [the longest x14 195 us: partner(): return lax.ppermute(block, axis, route)]
    ppermute x36 -> x0, starting transfers between devices: 231 us -> none  [the longest x22 122 us: shifted(): return lax.ppermute(block, axis, route)]
    pallas_call x0 -> x1, Pallas kernels: none -> 62.7 us  [per_device(): pl.pallas_call(body, out_shape=jax.ShapeDtypeStruct(queries.shape, querie...]
    unnamed x55 -> x9, local copies, waits for them, and re-layouts: 30 us -> 4.66 us
    all_to_all x1 -> x0, blocking collectives: 15.1 us -> none  [per_device(): lax.all_to_all(result, 'head', split_axis=1, concat_axis=2, tiled=True)]
    sub x8 -> x0, matrix products: 13.5 us -> none  [attend(): weights = jnp.where(allowed[None], jnp.exp(masked - top), 0.0)]
    all_to_all x3 -> x0, starting transfers between devices: 12.3 us -> none  [the longest x1 4.84 us: per_device(): lax.all_to_all(keys, 'head', split_axis=2, concat_axis=1, tiled=True)]
    all_to_all x7 -> x0, local copies, waits for them, and re-layouts: 12 us -> none  [the longest x1 9.82 us: per_device(): lax.all_to_all(queries, 'head', split_axis=2, concat_axis=1, tiled=True)]
  transfers between devices with their start and end apart: 39 -> 0, of which waited for: 20 -> 0; matrix products, arithmetic and copies ran while one was open for 7% -> 0% of each run, Pallas kernels for 0% -> 0%
where the time goes in v1:
time: 67.5 us; the launch traced here: 67.4 us
  Pallas kernels  62.7 us (93%)
  local copies, waits for them, and re-layouts  4.66 us (7%)
    pallas_call x1, Pallas kernels, per_device(): pl.pallas_call(body, out_shape=jax.ShapeDtypeStruct(queries.shape, querie...  62.7 us
    unnamed x9, local copies, waits for them, and re-layouts  4.66 us

profile of v1, /device:TPU:1, one launch (start us, length us, event | category | flops | bytes accessed | tf_op | source)
XLA Modules:
  0.0 67.4 jit_solution(8513659492173655465)
XLA Ops:
  0.0 0.0 copy-start
  0.0 1.2 %copy-done = bf16[2,32,8192]{2,1,0:T(8,128)(2,1)S(1)} copy-done((bf16[2,32,8192]{2,1,0:T(8,128)(2,1)S(1)}, bf16[2,32,8192]{2,1,0:T(8,128)(2,1)}, u32[]{:S(2)}) %copy-start) | copy-done | bytes 1048600
  1.2 0.0 copy-start.1
  1.2 0.9 %copy-done.1 = bf16[2,32,1024]{2,1,0:T(8,128)(2,1)S(1)} copy-done((bf16[2,32,1024]{2,1,0:T(8,128)(2,1)S(1)}, bf16[2,32,1024]{2,1,0:T(8,128)(2,1)}, u32[]{:S(2)}) %copy-start.1) | copy-done | bytes 131096
  2.1 0.0 copy-start.2
  2.1 0.9 %copy-done.2 = bf16[2,32,1024]{2,1,0:T(8,128)(2,1)S(1)} copy-done((bf16[2,32,1024]{2,1,0:T(8,128)(2,1)S(1)}, bf16[2,32,1024]{2,1,0:T(8,128)(2,1)}, u32[]{:S(2)}) %copy-start.2) | copy-done | bytes 131096
  3.0 0.0 copy-start.3
  3.0 0.7 copy-done.3
  3.7 62.7 %shard_map.46 = bf16[2,32,8192]{2,1,0:T(8,128)(2,1)S(1)} custom-call(bf16[2,32,8192]{2,1,0:T(8,128)(2,1)S(1)} %copy-done, bf16[2,32,1024]{2,1,0:T(8,128)(2,1)S(1)} %copy-done.1, bf16[2,32,1024]{2,1,0:T(8,128)(2,1)S(1)} %copy-done.2, s32[47]{0:T(128)S(1)} %copy-done.3), custom_call_target="tpu_custom_call" | custom-call | flops 3221225472 | bytes 5242880 | tf_op jit(solution)/shard_map/pallas_call | solution.py:245
  66.4 1.0 %copy.6 = bf16[2,32,8192]{2,1,0:T(8,128)(2,1)} copy(bf16[2,32,8192]{2,1,0:T(8,128)(2,1)S(1)} %shard_map.46) | data formatting | bytes 2097152
Async XLA Ops:
  0.0 1.2 %copy-start = (bf16[2,32,8192]{2,1,0:T(8,128)(2,1)S(1)}, bf16[2,32,8192]{2,1,0:T(8,128)(2,1)}, u32[]{:S(2)}) copy-start(bf16[2,32,8192]{2,1,0:T(8,128)(2,1)} %q_ref.1) | copy-start | bytes 3145732
  1.2 0.9 %copy-start.1 = (bf16[2,32,1024]{2,1,0:T(8,128)(2,1)S(1)}, bf16[2,32,1024]{2,1,0:T(8,128)(2,1)}, u32[]{:S(2)}) copy-start(bf16[2,32,1024]{2,1,0:T(8,128)(2,1)} %k_ref.1) | copy-start | bytes 393220
  2.1 0.9 %copy-start.2 = (bf16[2,32,1024]{2,1,0:T(8,128)(2,1)S(1)}, bf16[2,32,1024]{2,1,0:T(8,128)(2,1)}, u32[]{:S(2)}) copy-start(bf16[2,32,1024]{2,1,0:T(8,128)(2,1)} %v_ref.1) | copy-start | bytes 393220
  3.0 0.7 copy-start.3

commit v2 on v1

--- a/solution.py
+++ b/solution.py
@@ -16,6 +16,16 @@
 GROUP_SIZE = 8
 SLOTS = 7
 NEG_FILL = -1e30
+ORDER = (
+    ("up", 0, 0, 0), ("down", 0, 0, 0), ("up", 0, 0, 1), ("down", 0, 0, 1),
+    ("up", 0, 1, 0), ("down", 0, 1, 0), ("up", 0, 1, 1), ("down", 0, 1, 1),
+    ("up", 1, 0, 0), ("up", 1, 0, 1), ("up", 1, 1, 0), ("up", 1, 1, 1),
+    ("up", 2, 0, 0), ("up", 2, 0, 1), ("up", 2, 1, 0), ("up", 2, 1, 1),
+    ("down", 6, 0, 0), ("down", 6, 0, 1), ("down", 6, 1, 0), ("down", 6, 1, 1),
+    ("up", 3, 0, 0), ("up", 3, 0, 1), ("up", 3, 1, 0), ("up", 3, 1, 1),
+    ("down", 5, 0, 0), ("down", 5, 0, 1), ("down", 5, 1, 0), ("down", 5, 1, 1),
+    ("up", 4, 0, 0), ("down", 4, 0, 1), (), ("up", 4, 1, 0), ("down", 4, 1, 1),
+)
 FACTOR = 1.0 / math.sqrt(HD) * math.log2(math.e)
 
 
@@ -29,8 +39,10 @@
     len_ref,
     out_ref,
     q_all,
-    k_win,
-    v_win,
+    k_low,
+    k_high,
+    v_low,
+    v_high,
     o_all,
     bias,
     scores,
@@ -53,6 +65,8 @@
     own_row = (SLOTS - 1) * span
     window = (SLOTS - 2) * span + 2 * block
 
+    windows = ((k_low, k_high), (v_low, v_high))
+
     def member(index):
         return (group * 2 + index // SIDE, lax.rem(index, SIDE))
 
@@ -68,15 +82,16 @@
     pl.semaphore_wait(barrier, GROUP_SIZE + 3)
 
     my_rows = pl.ds(pl.multiple_of(own_row + me * rows, rows), rows)
-    for which, (src, dst) in enumerate(((k_ref, k_win), (v_ref, v_win))):
-        for half in range(2):
+    for half in range(2):
+        for which, src in enumerate((k_ref, v_ref)):
+            dst = windows[which][half]
             for k in range(GROUP_SIZE):
                 index = lax.rem(me + k, GROUP_SIZE)
                 cols = pl.ds(pl.multiple_of(index * HD, HD), HD)
                 if k:
                     pltpu.make_async_remote_copy(
                         src.at[half, :, cols],
-                        dst.at[half, my_rows, :],
+                        dst.at[my_rows, :],
                         sent.at[which],
                         own_sem.at[which, half],
                         device_id=member(index),
@@ -84,7 +99,7 @@
                     ).start()
                 else:
                     pltpu.make_async_copy(
-                        src.at[half, :, cols], dst.at[half, my_rows, :], own_sem.at[which, half]
+                        src.at[half, :, cols], dst.at[my_rows, :], own_sem.at[which, half]
                     ).start()
 
     q_rows = pl.ds(pl.multiple_of(me * rows, rows), rows)
@@ -108,27 +123,24 @@
         return pl.ds((SLOTS - 1 - slot) * span, span)
 
     def hop(which, half, from_slot, to_slot, step, sem):
-        ref = (k_win, v_win)[which]
         crossed = (group + step + groups) // groups - 1
-        to_half = lax.rem(half + crossed + 2, 2)
-        return pltpu.make_async_remote_copy(
-            ref.at[half, slot_rows(from_slot), :],
-            ref.at[to_half, slot_rows(to_slot), :],
-            chain_sent.at[which],
-            sem.at[to_half],
-            device_id=along(step),
-            device_id_type=MESH,
-        )
+
+        def to(to_half):
+            pltpu.make_async_remote_copy(
+                windows[which][half].at[slot_rows(from_slot), :],
+                windows[which][to_half].at[slot_rows(to_slot), :],
+                chain_sent.at[which, half],
+                sem.at[to_half],
+                device_id=along(step),
+                device_id_type=MESH,
+            ).start()
+
+        pl.when(crossed == 0)(lambda: to(half))
+        pl.when(crossed != 0)(lambda: to(1 - half))
 
     def arrived(which, half, slot, sem):
-        ref = (k_win, v_win)[which].at[half, slot_rows(slot), :]
+        ref = windows[which][half].at[slot_rows(slot), :]
         pltpu.make_async_copy(ref, ref, sem.at[half]).wait()
-
-    for which in range(2):
-        for half in range(2):
-            arrived(which, half, 0, own_sem.at[which])
-            hop(which, half, 0, 1, 1, up_sem.at[0, which]).start()
-            hop(which, half, 0, 6, 6, down_sem.at[0, which]).start()
 
     for half in range(2):
         for part in range(2):
@@ -145,16 +157,23 @@
             allowed = (key_pos >= begin) & (key_pos <= pos)
             bias[half * 2 + part] = jnp.where(allowed, 0.0, NEG_FILL)
 
-    for step in range(3):
-        for which in range(2):
-            for half in range(2):
-                arrived(which, half, step + 1, up_sem.at[step, which])
-                if step < 2 or which == 0:
-                    hop(which, half, step + 1, step + 2, 1, up_sem.at[step + 1, which]).start()
-                if step < 2:
-                    arrived(which, half, 6 - step, down_sem.at[step, which])
-                    if step == 0 or which == 1:
-                        hop(which, half, 6 - step, 5 - step, -1, down_sem.at[step + 1, which]).start()
+    awaited = set()
+
+    def pass_on(way, slot, half, which):
+        if slot == 0 and (half, which) not in awaited:
+            awaited.add((half, which))
+            arrived(which, half, 0, own_sem.at[which])
+        if way == "up":
+            if slot > 0:
+                arrived(which, half, slot, up_sem.at[slot - 1, which])
+            if slot < 3 or (slot == 3 and which == 0):
+                hop(which, half, slot, slot + 1, 1, up_sem.at[slot, which])
+        elif slot == 0:
+            hop(which, half, 0, 6, 6, down_sem.at[0, which])
+        else:
+            arrived(which, half, slot, down_sem.at[6 - slot, which])
+            if slot == 6 or (slot == 5 and which == 1):
+                hop(which, half, slot, slot - 1, -1, down_sem.at[7 - slot, which])
 
     def unit(u, half):
         part = u // 2
@@ -169,7 +188,7 @@
             ],
             axis=0,
         )
-        keys = k_win[half, pl.ds(keys_from, window), :]
+        keys = windows[0][half][pl.ds(keys_from, window), :]
         for tile in range(window // 256):
             part_keys = keys[tile * 256 : (tile + 1) * 256]
             product = lax.dot_general(
@@ -179,7 +198,7 @@
             scores[:, tile * 256 : (tile + 1) * 256] = (
                 product.reshape(GROUP // 2, block, 256) + add[None]
             ).reshape(GROUP // 2 * block, 256)
-        values = v_win[half, pl.ds(keys_from, window), :]
+        values = windows[1][half][pl.ds(keys_from, window), :]
         values = jnp.concatenate([values, jnp.ones_like(values)], axis=1)
         for i in range(GROUP // 2):
             s = scores[i * block : (i + 1) * block, :]
@@ -213,12 +232,14 @@
 
         return 0
 
-    for half in range(2):
-        pltpu.make_async_copy(q_all.at[half], q_all.at[half], q_sem.at[half]).wait()
-        arrived(0, half, 4, up_sem.at[3, 0])
-        arrived(1, half, 4, down_sem.at[2, 1])
-    for half in range(2):
-        lax.fori_loop(0, 4, lambda u, _, half=half: unit(u, half), 0)
+    for entry in ORDER:
+        if entry:
+            pass_on(*entry)
+        else:
+            for half in range(2):
+                pltpu.make_async_copy(q_all.at[half], q_all.at[half], q_sem.at[half]).wait()
+            lax.fori_loop(0, 4, lambda u, _: unit(u, 0), 0)
+    lax.fori_loop(0, 4, lambda u, _: unit(u, 1), 0)
 
     pltpu.make_async_copy(out_ref, out_ref, out_sem).wait()
     others = k_ref.at[:, :, : (GROUP_SIZE - 1) * HD]
@@ -228,8 +249,9 @@
     pltpu.make_async_copy(others, others, sent.at[2]).wait()
     pltpu.make_async_copy(others, others, sent.at[3]).wait()
     for which in range(2):
-        hops = (k_win, v_win)[which].at[:, pl.ds(0, 6 * span), :]
-        pltpu.make_async_copy(hops, hops, chain_sent.at[which]).wait()
+        for half in range(2):
+            hops = windows[which][half].at[pl.ds(0, 6 * span), :]
+            pltpu.make_async_copy(hops, hops, chain_sent.at[which, half]).wait()
 
 
 def per_device(queries, keys, values, doc_lengths):
@@ -249,8 +271,10 @@
         out_specs=anywhere,
         scratch_shapes=[
             pltpu.VMEM((2, span, GROUP * HD), jnp.bfloat16),
-            pltpu.VMEM((2, SLOTS * span, HD), jnp.bfloat16),
-            pltpu.VMEM((2, SLOTS * span, HD), jnp.bfloat16),
+            pltpu.VMEM((SLOTS * span, HD), jnp.bfloat16),
+            pltpu.VMEM((SLOTS * span, HD), jnp.bfloat16),
+            pltpu.VMEM((SLOTS * span, HD), jnp.bfloat16),
+            pltpu.VMEM((SLOTS * span, HD), jnp.bfloat16),
             pltpu.VMEM((8, block, GROUP // 2 * HD), jnp.bfloat16),
             pltpu.VMEM((4, block, window), jnp.float32),
             pltpu.VMEM((GROUP // 2 * block, window), jnp.float32),
@@ -259,11 +283,11 @@
             pltpu.SemaphoreType.DMA((2,)),
             pltpu.SemaphoreType.DMA((4, 2, 2)),
             pltpu.SemaphoreType.DMA((3, 2, 2)),
-            pltpu.SemaphoreType.DMA((2,)),
+            pltpu.SemaphoreType.DMA((2, 2)),
             pltpu.SemaphoreType.DMA,
         ],
         compiler_params=pltpu.CompilerParams(
-            collective_id=0, has_side_effects=True, vmem_limit_bytes=48 << 20
+            collective_id=0, has_side_effects=True, vmem_limit_bytes=63 << 20
         ),
         cost_estimate=pl.CostEstimate(
             flops=4 * pairs * window * HD, bytes_accessed=5 << 20, transcendentals=pairs * window

time: 67.5 us -> 66.8 us (0.990)
  local copies, waits for them, and re-layouts: 4.66 us -> 2.26 us
  Pallas kernels: 62.7 us -> 64.3 us
    unnamed x9 -> x1, local copies, waits for them, and re-layouts: 4.66 us -> 2.26 us
    pallas_call x1, Pallas kernels: 62.7 us -> 64.3 us  [per_device(): pl.pallas_call(body, out_shape=jax.ShapeDtypeStruct(queries.shape, querie...]
where the time goes in v2:
time: 66.8 us; the launch traced here: 66.6 us
  Pallas kernels  64.3 us (96%)
  local copies, waits for them, and re-layouts  2.26 us (3%)
    pallas_call x1, Pallas kernels, per_device(): pl.pallas_call(body, out_shape=jax.ShapeDtypeStruct(queries.shape, querie...  64.3 us
    unnamed x1, local copies, waits for them, and re-layouts  2.26 us

profile of v2, /device:TPU:1, one launch (start us, length us, event | category | flops | bytes accessed | tf_op | source)
XLA Modules:
  0.0 66.6 jit_solution(17738466151038891924)
XLA Ops:
  0.0 64.3 %shard_map.46 = bf16[2,32,8192]{2,1,0:T(8,128)(2,1)} custom-call(bf16[2,32,8192]{2,1,0:T(8,128)(2,1)} %q_ref.1, bf16[2,32,1024]{2,1,0:T(8,128)(2,1)} %k_ref.1, bf16[2,32,1024]{2,1,0:T(8,128)(2,1)} %v_ref.1, s32[47]{0:T(128)} %len_ref.1), custom_call_target="tpu_custom_call" | custom-call | flops 3221225472 | bytes 5242880 | tf_op jit(solution)/shard_map/pallas_call | solution.py:267
  64.3 2.3 %copy.6 = bf16[2,32,8192]{2,1,0:T(8,128)(2,1)} copy(bf16[2,32,8192]{2,1,0:T(8,128)(2,1)} %shard_map.46) | data formatting | bytes 2097152

commit v3 on v2

--- a/solution.py
+++ b/solution.py
@@ -15,11 +15,13 @@
 SIDE = 4
 GROUP_SIZE = 8
 SLOTS = 7
+RING = 8
 NEG_FILL = -1e30
 ORDER = (
     ("up", 0, 0, 0), ("down", 0, 0, 0), ("up", 0, 0, 1), ("down", 0, 0, 1),
     ("up", 0, 1, 0), ("down", 0, 1, 0), ("up", 0, 1, 1), ("down", 0, 1, 1),
     ("up", 1, 0, 0), ("up", 1, 0, 1), ("up", 1, 1, 0), ("up", 1, 1, 1),
+    ("relay", 0, 0, 0), ("relay", 0, 0, 1), ("relay", 0, 1, 0), ("relay", 0, 1, 1),
     ("up", 2, 0, 0), ("up", 2, 0, 1), ("up", 2, 1, 0), ("up", 2, 1, 1),
     ("down", 6, 0, 0), ("down", 6, 0, 1), ("down", 6, 1, 0), ("down", 6, 1, 1),
     ("up", 3, 0, 0), ("up", 3, 0, 1), ("up", 3, 1, 0), ("up", 3, 1, 1),
@@ -43,6 +45,7 @@
     k_high,
     v_low,
     v_high,
+    relayed,
     o_all,
     bias,
     scores,
@@ -52,12 +55,15 @@
     up_sem,
     down_sem,
     chain_sent,
+    relay_sem,
+    relay_sent,
     out_sem,
 ):
     ctx = lax.axis_index("ctx")
     x = lax.axis_index("head")
     core = lax.rem(ctx, 2)
     group = ctx // 2
+    place = lax.rem(group, RING)
     me = core * SIDE + x
     span = rows * GROUP_SIZE
     block = span // 2
@@ -77,9 +83,9 @@
     for k in range(1, GROUP_SIZE):
         other = member(lax.rem(me + k, GROUP_SIZE))
         pl.semaphore_signal(barrier, inc=1, device_id=other, device_id_type=MESH)
-    for step in (1, -1, SLOTS - 1, 1 - SLOTS):
+    for step in (1, -1, SLOTS - 1, 1 - SLOTS, SLOTS, -SLOTS):
         pl.semaphore_signal(barrier, inc=1, device_id=along(step), device_id_type=MESH)
-    pl.semaphore_wait(barrier, GROUP_SIZE + 3)
+    pl.semaphore_wait(barrier, GROUP_SIZE + 5)
 
     my_rows = pl.ds(pl.multiple_of(own_row + me * rows, rows), rows)
     for half in range(2):
@@ -122,14 +128,14 @@
     def slot_rows(slot):
         return pl.ds((SLOTS - 1 - slot) * span, span)
 
-    def hop(which, half, from_slot, to_slot, step, sem):
+    def hop(which, half, source, to_slot, step, sem, left):
         crossed = (group + step + groups) // groups - 1
 
         def to(to_half):
             pltpu.make_async_remote_copy(
-                windows[which][half].at[slot_rows(from_slot), :],
+                source,
                 windows[which][to_half].at[slot_rows(to_slot), :],
-                chain_sent.at[which, half],
+                left.at[which, half],
                 sem.at[to_half],
                 device_id=along(step),
                 device_id_type=MESH,
@@ -160,6 +166,7 @@
     awaited = set()
 
     def pass_on(way, slot, half, which):
+        source = windows[which][half].at[slot_rows(slot), :]
         if slot == 0 and (half, which) not in awaited:
             awaited.add((half, which))
             arrived(which, half, 0, own_sem.at[which])
@@ -167,13 +174,36 @@
             if slot > 0:
                 arrived(which, half, slot, up_sem.at[slot - 1, which])
             if slot < 3 or (slot == 3 and which == 0):
-                hop(which, half, slot, slot + 1, 1, up_sem.at[slot, which])
+                hop(which, half, source, slot + 1, 1, up_sem.at[slot, which], chain_sent)
+        elif way == "relay":
+
+            @pl.when(place == RING - 2)
+            def _():
+                ref = relayed.at[which, half]
+                pltpu.make_async_copy(ref, ref, relay_sem.at[which, half]).wait()
+                hop(which, half, ref, SLOTS - 1, SLOTS, down_sem.at[0, which], relay_sent)
+
         elif slot == 0:
-            hop(which, half, 0, 6, 6, down_sem.at[0, which])
+
+            @pl.when(place != RING - 1)
+            def _():
+                hop(which, half, source, SLOTS - 1, SLOTS - 1, down_sem.at[0, which], chain_sent)
+
+            @pl.when(place == RING - 1)
+            def _():
+                pltpu.make_async_remote_copy(
+                    source,
+                    relayed.at[which, half],
+                    chain_sent.at[which, half],
+                    relay_sem.at[which, half],
+                    device_id=along(-1),
+                    device_id_type=MESH,
+                ).start()
+
         else:
             arrived(which, half, slot, down_sem.at[6 - slot, which])
             if slot == 6 or (slot == 5 and which == 1):
-                hop(which, half, slot, slot - 1, -1, down_sem.at[7 - slot, which])
+                hop(which, half, source, slot - 1, -1, down_sem.at[7 - slot, which], chain_sent)
 
     def unit(u, half):
         part = u // 2
@@ -253,6 +283,11 @@
             hops = windows[which][half].at[pl.ds(0, 6 * span), :]
             pltpu.make_async_copy(hops, hops, chain_sent.at[which, half]).wait()
 
+            @pl.when(place == RING - 2)
+            def _(which=which, half=half):
+                ref = relayed.at[which, half]
+                pltpu.make_async_copy(ref, ref, relay_sent.at[which, half]).wait()
+
 
 def per_device(queries, keys, values, doc_lengths):
     rows = queries.shape[1]
@@ -275,6 +310,7 @@
             pltpu.VMEM((SLOTS * span, HD), jnp.bfloat16),
             pltpu.VMEM((SLOTS * span, HD), jnp.bfloat16),
             pltpu.VMEM((SLOTS * span, HD), jnp.bfloat16),
+            pltpu.VMEM((2, 2, span, HD), jnp.bfloat16),
             pltpu.VMEM((8, block, GROUP // 2 * HD), jnp.bfloat16),
             pltpu.VMEM((4, block, window), jnp.float32),
             pltpu.VMEM((GROUP // 2 * block, window), jnp.float32),
@@ -283,6 +319,8 @@
             pltpu.SemaphoreType.DMA((2,)),
             pltpu.SemaphoreType.DMA((4, 2, 2)),
             pltpu.SemaphoreType.DMA((3, 2, 2)),
+            pltpu.SemaphoreType.DMA((2, 2)),
+            pltpu.SemaphoreType.DMA((2, 2)),
             pltpu.SemaphoreType.DMA((2, 2)),
             pltpu.SemaphoreType.DMA,
         ],

time: 66.8 us -> 61.2 us (0.916)
  Pallas kernels: 64.3 us -> 58.8 us
    pallas_call x1, Pallas kernels: 64.3 us -> 58.8 us  [per_device(): pl.pallas_call(body, out_shape=jax.ShapeDtypeStruct(queries.shape, querie...]
where the time goes in v3:
time: 61.2 us; the launch traced here: 61 us
  Pallas kernels  58.8 us (96%)
  local copies, waits for them, and re-layouts  2.26 us (4%)
    pallas_call x1, Pallas kernels, per_device(): pl.pallas_call(body, out_shape=jax.ShapeDtypeStruct(queries.shape, querie...  58.8 us
    unnamed x1, local copies, waits for them, and re-layouts  2.26 us

profile of v3, /device:TPU:1, one launch (start us, length us, event | category | flops | bytes accessed | tf_op | source)
XLA Modules:
  0.0 61.0 jit_solution(17326293571639604215)
XLA Ops:
  0.0 58.8 %shard_map.46 = bf16[2,32,8192]{2,1,0:T(8,128)(2,1)} custom-call(bf16[2,32,8192]{2,1,0:T(8,128)(2,1)} %q_ref.1, bf16[2,32,1024]{2,1,0:T(8,128)(2,1)} %k_ref.1, bf16[2,32,1024]{2,1,0:T(8,128)(2,1)} %v_ref.1, s32[47]{0:T(128)} %len_ref.1), custom_call_target="tpu_custom_call" | custom-call | flops 3221225472 | bytes 5242880 | tf_op jit(solution)/shard_map/pallas_call | solution.py:302
  58.8 2.3 %copy.6 = bf16[2,32,8192]{2,1,0:T(8,128)(2,1)} copy(bf16[2,32,8192]{2,1,0:T(8,128)(2,1)} %shard_map.46) | data formatting | bytes 2097152

commit v4 on v3

--- a/solution.py
+++ b/solution.py
@@ -15,17 +15,18 @@
 SIDE = 4
 GROUP_SIZE = 8
 SLOTS = 7
+OWN = 8
 RING = 8
 NEG_FILL = -1e30
 ORDER = (
-    ("up", 0, 0, 0), ("down", 0, 0, 0), ("up", 0, 0, 1), ("down", 0, 0, 1),
-    ("up", 0, 1, 0), ("down", 0, 1, 0), ("up", 0, 1, 1), ("down", 0, 1, 1),
-    ("up", 1, 0, 0), ("up", 1, 0, 1), ("up", 1, 1, 0), ("up", 1, 1, 1),
-    ("relay", 0, 0, 0), ("relay", 0, 0, 1), ("relay", 0, 1, 0), ("relay", 0, 1, 1),
-    ("up", 2, 0, 0), ("up", 2, 0, 1), ("up", 2, 1, 0), ("up", 2, 1, 1),
-    ("down", 6, 0, 0), ("down", 6, 0, 1), ("down", 6, 1, 0), ("down", 6, 1, 1),
-    ("up", 3, 0, 0), ("up", 3, 0, 1), ("up", 3, 1, 0), ("up", 3, 1, 1),
-    ("down", 5, 0, 0), ("down", 5, 0, 1), ("down", 5, 1, 0), ("down", 5, 1, 1),
+    ("up", 0, 0, 0), ("up", 0, 1, 0), ("down", 0, 0, 0), ("down", 0, 1, 0),
+    ("up", 0, 0, 1), ("up", 0, 1, 1), ("down", 0, 0, 1), ("down", 0, 1, 1),
+    ("up", 1, 0, 0), ("up", 1, 1, 0), ("up", 1, 0, 1), ("up", 1, 1, 1),
+    ("up", 2, 0, 0), ("up", 2, 1, 0), ("up", 2, 0, 1), ("up", 2, 1, 1),
+    ("relay", 0, 0, 0), ("relay", 0, 1, 0), ("relay", 0, 0, 1), ("relay", 0, 1, 1),
+    ("down", 6, 0, 0), ("down", 6, 1, 0), ("down", 6, 0, 1), ("down", 6, 1, 1),
+    ("up", 3, 0, 0), ("up", 3, 1, 0), ("up", 3, 0, 1), ("up", 3, 1, 1),
+    ("down", 5, 0, 0), ("down", 5, 1, 0), ("down", 5, 0, 1), ("down", 5, 1, 1),
     ("up", 4, 0, 0), ("down", 4, 0, 1), (), ("up", 4, 1, 0), ("down", 4, 1, 1),
 )
 FACTOR = 1.0 / math.sqrt(HD) * math.log2(math.e)
@@ -88,8 +89,8 @@
     pl.semaphore_wait(barrier, GROUP_SIZE + 5)
 
     my_rows = pl.ds(pl.multiple_of(own_row + me * rows, rows), rows)
-    for half in range(2):
-        for which, src in enumerate((k_ref, v_ref)):
+    for which, src in enumerate((k_ref, v_ref)):
+        for half in range(2):
             dst = windows[which][half]
             for k in range(GROUP_SIZE):
                 index = lax.rem(me + k, GROUP_SIZE)
@@ -108,6 +109,74 @@
                         src.at[half, :, cols], dst.at[my_rows, :], own_sem.at[which, half]
                     ).start()
 
+    def slot_rows(slot):
+        return pl.ds((SLOTS - 1 - slot) * span, span)
+
+    def hop(which, half, source, to_slot, step, sem, left):
+        crossed = (group + step + groups) // groups - 1
+
+        def to(to_half):
+            pltpu.make_async_remote_copy(
+                source,
+                windows[which][to_half].at[slot_rows(to_slot), :],
+                left.at[which, half],
+                sem.at[to_half],
+                device_id=along(step),
+                device_id_type=MESH,
+            ).start()
+
+        pl.when(crossed == 0)(lambda: to(half))
+        pl.when(crossed != 0)(lambda: to(1 - half))
+
+    def arrived(which, half, slot, sem):
+        ref = windows[which][half].at[slot_rows(slot), :]
+        pltpu.make_async_copy(ref, ref, sem.at[half]).wait()
+
+    awaited = set()
+
+    def pass_on(way, slot, half, which):
+        source = windows[which][half].at[slot_rows(slot), :]
+        if slot == 0 and (half, which) not in awaited:
+            awaited.add((half, which))
+            arrived(which, half, 0, own_sem.at[which])
+        if way == "up":
+            if slot > 0:
+                arrived(which, half, slot, up_sem.at[slot - 1, which])
+            if slot < 3 or (slot == 3 and which == 0):
+                hop(which, half, source, slot + 1, 1, up_sem.at[slot, which], chain_sent)
+        elif way == "relay":
+
+            @pl.when(place == RING - 2)
+            def _():
+                ref = relayed.at[which, half]
+                pltpu.make_async_copy(ref, ref, relay_sem.at[which, half]).wait()
+                hop(which, half, ref, SLOTS - 1, SLOTS, down_sem.at[0, which], relay_sent)
+
+        elif slot == 0:
+
+            @pl.when(place != RING - 1)
+            def _():
+                hop(which, half, source, SLOTS - 1, SLOTS - 1, down_sem.at[0, which], chain_sent)
+
+            @pl.when(place == RING - 1)
+            def _():
+                pltpu.make_async_remote_copy(
+                    source,
+                    relayed.at[which, half],
+                    chain_sent.at[which, half],
+                    relay_sem.at[which, half],
+                    device_id=along(-1),
+                    device_id_type=MESH,
+                ).start()
+
+        else:
+            arrived(which, half, slot, down_sem.at[6 - slot, which])
+            if slot == 6 or (slot == 5 and which == 1):
+                hop(which, half, source, slot - 1, -1, down_sem.at[7 - slot, which], chain_sent)
+
+    for entry in ORDER[:OWN]:
+        pass_on(*entry)
+
     q_rows = pl.ds(pl.multiple_of(me * rows, rows), rows)
     for half in range(2):
         for k in range(GROUP_SIZE):
@@ -125,29 +194,6 @@
             else:
                 pltpu.make_async_copy(q_ref.at[half, :, cols], q_all.at[half, q_rows, :], q_sem.at[half]).start()
 
-    def slot_rows(slot):
-        return pl.ds((SLOTS - 1 - slot) * span, span)
-
-    def hop(which, half, source, to_slot, step, sem, left):
-        crossed = (group + step + groups) // groups - 1
-
-        def to(to_half):
-            pltpu.make_async_remote_copy(
-                source,
-                windows[which][to_half].at[slot_rows(to_slot), :],
-                left.at[which, half],
-                sem.at[to_half],
-                device_id=along(step),
-                device_id_type=MESH,
-            ).start()
-
-        pl.when(crossed == 0)(lambda: to(half))
-        pl.when(crossed != 0)(lambda: to(1 - half))
-
-    def arrived(which, half, slot, sem):
-        ref = windows[which][half].at[slot_rows(slot), :]
-        pltpu.make_async_copy(ref, ref, sem.at[half]).wait()
-
     for half in range(2):
         for part in range(2):
             first = half * half_len + group * span + part * block
@@ -162,48 +208,6 @@
             key_pos = first - (window - block) + lax.broadcasted_iota(jnp.int32, (1, window), 1)
             allowed = (key_pos >= begin) & (key_pos <= pos)
             bias[half * 2 + part] = jnp.where(allowed, 0.0, NEG_FILL)
-
-    awaited = set()
-
-    def pass_on(way, slot, half, which):
-        source = windows[which][half].at[slot_rows(slot), :]
-        if slot == 0 and (half, which) not in awaited:
-            awaited.add((half, which))
-            arrived(which, half, 0, own_sem.at[which])
-        if way == "up":
-            if slot > 0:
-                arrived(which, half, slot, up_sem.at[slot - 1, which])
-            if slot < 3 or (slot == 3 and which == 0):
-                hop(which, half, source, slot + 1, 1, up_sem.at[slot, which], chain_sent)
-        elif way == "relay":
-
-            @pl.when(place == RING - 2)
-            def _():
-                ref = relayed.at[which, half]
-                pltpu.make_async_copy(ref, ref, relay_sem.at[which, half]).wait()
-                hop(which, half, ref, SLOTS - 1, SLOTS, down_sem.at[0, which], relay_sent)
-
-        elif slot == 0:
-
-            @pl.when(place != RING - 1)
-            def _():
-                hop(which, half, source, SLOTS - 1, SLOTS - 1, down_sem.at[0, which], chain_sent)
-
-            @pl.when(place == RING - 1)
-            def _():
-                pltpu.make_async_remote_copy(
-                    source,
-                    relayed.at[which, half],
-                    chain_sent.at[which, half],
-                    relay_sem.at[which, half],
-                    device_id=along(-1),
-                    device_id_type=MESH,
-                ).start()
-
-        else:
-            arrived(which, half, slot, down_sem.at[6 - slot, which])
-            if slot == 6 or (slot == 5 and which == 1):
-                hop(which, half, source, slot - 1, -1, down_sem.at[7 - slot, which], chain_sent)
 
     def unit(u, half):
         part = u // 2
@@ -262,7 +266,7 @@
 
         return 0
 
-    for entry in ORDER:
+    for entry in ORDER[OWN:]:
         if entry:
             pass_on(*entry)
         else:

time: 61.2 us -> 60.3 us (0.985)
  Pallas kernels: 58.8 us -> 57.6 us
    pallas_call x1, Pallas kernels: 58.8 us -> 57.6 us  [per_device(): pl.pallas_call(body, out_shape=jax.ShapeDtypeStruct(queries.shape, querie...]
where the time goes in v4:
time: 60.3 us; the launch traced here: 59.9 us
  Pallas kernels  57.6 us (96%)
  local copies, waits for them, and re-layouts  2.26 us (4%)
    pallas_call x1, Pallas kernels, per_device(): pl.pallas_call(body, out_shape=jax.ShapeDtypeStruct(queries.shape, querie...  57.6 us
    unnamed x1, local copies, waits for them, and re-layouts  2.26 us

profile of v4, /device:TPU:1, one launch (start us, length us, event | category | flops | bytes accessed | tf_op | source)
XLA Modules:
  0.0 59.9 jit_solution(2800122992907665205)
XLA Ops:
  0.0 57.6 %shard_map.46 = bf16[2,32,8192]{2,1,0:T(8,128)(2,1)} custom-call(bf16[2,32,8192]{2,1,0:T(8,128)(2,1)} %q_ref.1, bf16[2,32,1024]{2,1,0:T(8,128)(2,1)} %k_ref.1, bf16[2,32,1024]{2,1,0:T(8,128)(2,1)} %v_ref.1, s32[47]{0:T(128)} %len_ref.1), custom_call_target="tpu_custom_call" | custom-call | flops 3221225472 | bytes 5242880 | tf_op jit(solution)/shard_map/pallas_call | solution.py:306
  57.6 2.3 %copy.6 = bf16[2,32,8192]{2,1,0:T(8,128)(2,1)} copy(bf16[2,32,8192]{2,1,0:T(8,128)(2,1)} %shard_map.46) | data formatting | bytes 2097152

commit v5 on v4

--- a/solution.py
+++ b/solution.py
@@ -240,7 +240,7 @@
             weight = jnp.exp2((s - top) * FACTOR).astype(jnp.bfloat16)
             mixed = jnp.dot(weight, values, preferred_element_type=jnp.float32)
             o_all[half * 4 + u, :, i * HD : (i + 1) * HD] = (mixed[:, :HD] / mixed[:, HD:]).astype(jnp.bfloat16)
-        for k in range(SIDE):
+        for k in (2, 1, 3, 0):
             to_x = lax.rem(x + k, SIDE)
             src = o_all.at[half * 4 + u, pl.ds(pl.multiple_of(to_x * rows, rows), rows), :]
             dst = out_ref.at[half, :, pl.ds(pl.multiple_of(me * wide + col0, wide // 2), wide // 2)]

time: 60.3 us -> 60.2 us (level)
  no operation moved by 1% of the time
where the time goes in v5:
time: 60.2 us; the launch traced here: 59.7 us
  Pallas kernels  57.4 us (95%)
  local copies, waits for them, and re-layouts  2.26 us (4%)
    pallas_call x1, Pallas kernels, per_device(): pl.pallas_call(body, out_shape=jax.ShapeDtypeStruct(queries.shape, querie...  57.4 us
    unnamed x1, local copies, waits for them, and re-layouts  2.26 us

profile of v5, /device:TPU:1, one launch (start us, length us, event | category | flops | bytes accessed | tf_op | source)
XLA Modules:
  0.0 59.7 jit_solution(3058886312077025671)
XLA Ops:
  0.0 57.4 %shard_map.46 = bf16[2,32,8192]{2,1,0:T(8,128)(2,1)} custom-call(bf16[2,32,8192]{2,1,0:T(8,128)(2,1)} %q_ref.1, bf16[2,32,1024]{2,1,0:T(8,128)(2,1)} %k_ref.1, bf16[2,32,1024]{2,1,0:T(8,128)(2,1)} %v_ref.1, s32[47]{0:T(128)} %len_ref.1), custom_call_target="tpu_custom_call" | custom-call | flops 3221225472 | bytes 5242880 | tf_op jit(solution)/shard_map/pallas_call | solution.py:306
  57.4 2.3 %copy.6 = bf16[2,32,8192]{2,1,0:T(8,128)(2,1)} copy(bf16[2,32,8192]{2,1,0:T(8,128)(2,1)} %shard_map.46) | data formatting | bytes 2097152
